TPU v7x, 512 devices: a whole 4x4x16 slice. The times are simulated.
512 devices in a mesh: space: 128 (over z, x, core), basis: 4 (over y).
Axes of the slice: x: 4, y: 4, z: 16, core: 2. Of those that a mesh axis runs over, the one named last changes fastest.
Arguments:
- x_block: float32 [16, 3, 128, 32, 128], P(None, None, 'space', 'basis'), may hold values from -68 to 68
- basis: float32 [64, 3, 128, 32, 128], P('basis', None, 'space'), may hold values from -11 to 11
- material: int32 [128, 32, 128], P('space', 'basis'), may hold values from 0 to 7
- k0_blocks: float32 [8, 7, 3, 3], replicated, may hold values from -4 to 4
- k0_diag: float32 [8, 3], replicated, may hold values from 2 to 8
- ke_blocks: float32 [8, 7, 3, 3], replicated, may hold values from -6 to 6
- mass: float32 [8, 3], replicated, may hold values from 0.5 to 2
- velocities: float32 [1024], replicated, may hold values from 0.5 to 1
- shifts: float32 [1024], replicated, may hold values from 0.5 to 1.5
- sample: int32 [1], replicated, may hold values from 0 to 1023
Outputs:
- orthonormal: float32 [16, 3, 128, 32, 128], P(None, None, 'space', 'basis')
- coefficients: float32 [64, 16], P('basis')
- upper_factor: float32 [16, 16], replicated
All inputs are finite; a program needn't handle non-finite values.
Results may differ from a plain program's by a relative error of at most 0.00015.
Values sent between devices are 32-bit elements; how exact they have to be, the bound alone decides.
A program may use at most 64 MiB of HBM per device.

v0:
```python
import jax
import jax.numpy as jnp
from jax import lax
from jax.sharding import PartitionSpec as P

exact_precision = lax.Precision.HIGHEST


def with_halo(cells, sides, width):
    for axis, dim in sides:
        count = lax.axis_size(axis)
        ends = count - 1
        head = lax.slice_in_dim(cells, 0, width, axis=dim)
        tail = lax.slice_in_dim(cells, cells.shape[dim] - width, cells.shape[dim], axis=dim)
        cells = jnp.concatenate(
            [
                lax.ppermute(tail, axis, [(i, (i + 1) % count) for i in range(ends)]),
                cells,
                lax.ppermute(head, axis, [((i + 1) % count, i) for i in range(ends)]),
            ],
            axis=dim,
        )
    return cells


def stencil_tables(k0_blocks, k0_diag, ke_blocks, mass, velocities, shifts, sample):
    velocity = jnp.take(velocities, sample, axis=0)[0]
    sigma_value = jnp.take(shifts, sample, axis=0)[0]
    center = (k0_diag - sigma_value * mass)[:, :, None] * jnp.eye(3, dtype=jnp.float32)
    tables = k0_blocks - velocity * velocity * ke_blocks
    return tables.at[:, 0].add(center)


def neighbour_views(rimmed):
    centre = rimmed[:, :, 1:-1, 1:-1, :]
    lower_x = rimmed[:, :, :-2, 1:-1, :]
    upper_x = rimmed[:, :, 2:, 1:-1, :]
    lower_y = rimmed[:, :, 1:-1, :-2, :]
    upper_y = rimmed[:, :, 1:-1, 2:, :]
    zero_col = jnp.zeros(centre.shape[:4] + (1,), centre.dtype)
    lower_z = jnp.concatenate((zero_col, centre[:, :, :, :, :-1]), axis=4)
    upper_z = jnp.concatenate((centre[:, :, :, :, 1:], zero_col), axis=4)
    return [centre, lower_x, upper_x, lower_y, upper_y, lower_z, upper_z]


def cell_fields(tables, material_cells):
    material_count = tables.shape[0]
    fields = jnp.zeros((7, 3, 3) + material_cells.shape, jnp.float32)
    for level in range(material_count):
        chosen = (material_cells == level).astype(jnp.float32)
        fields = fields + tables[level][:, :, :, None, None, None] * chosen[None, None, None]
    return fields


def apply_fields(rimmed, fields):
    stencil_views = neighbour_views(rimmed)
    sums = [None, None, None]
    for offset in range(7):
        view = stencil_views[offset]
        for row in range(3):
            term = fields[offset, row, 0][None] * view[:, 0]
            term = term + fields[offset, row, 1][None] * view[:, 1]
            term = term + fields[offset, row, 2][None] * view[:, 2]
            sums[row] = term if sums[row] is None else sums[row] + term
    return jnp.stack(sums, axis=1)


def fine_image(x_block, material, tables):
    rimmed = with_halo(x_block, (("space", 2), ("basis", 3)), 1)
    return apply_fields(rimmed, cell_fields(tables, material))


def group_sum(partial_value):
    return lax.psum(partial_value, "space")


def scaled_block(fine_block, gram_matrix):
    block_cols = fine_block.shape[0]
    lower_factor = jnp.linalg.cholesky(gram_matrix)
    inverse = jax.scipy.linalg.solve_triangular(
        lower_factor, jnp.eye(block_cols, dtype=jnp.float32), lower=True
    ).T
    orthonormal = jnp.einsum("mcxyz,mn->ncxyz", fine_block, inverse, precision=exact_precision)
    return (orthonormal, lower_factor.T)


def finish(fine_block, row_count):
    gram_partial = jnp.einsum("ncxyz,mcxyz->nm", fine_block, fine_block, precision=exact_precision)
    gram_matrix = lax.psum(gram_partial, ("space", "basis")) / row_count
    return scaled_block(fine_block, gram_matrix)


def shards(
    x_block, basis, material, k0_blocks, k0_diag, ke_blocks, mass, velocities, shifts, sample
):
    tables = stencil_tables(k0_blocks, k0_diag, ke_blocks, mass, velocities, shifts, sample)
    block_cols = x_block.shape[0]
    extent_x = x_block.shape[2]
    extent_z = x_block.shape[4]
    full_y = basis.shape[3]
    group_cols = basis.shape[0]
    row_count = 3.0 * extent_x * lax.axis_size("space") * full_y * extent_z
    running = jnp.zeros((group_cols, block_cols), jnp.float32)
    fine_block = fine_image(x_block, material, tables)
    for repeat in range(2):
        partial_value = jnp.einsum(
            "kcxyz,ncxyz->kn",
            basis,
            lax.all_gather(fine_block, "basis", axis=3, tiled=True),
            precision=exact_precision,
        )
        local_coeffs = group_sum(partial_value) / row_count
        correction = jnp.einsum("kcxyz,kn->ncxyz", basis, local_coeffs, precision=exact_precision)
        fine_block = fine_block - lax.psum_scatter(
            correction, "basis", scatter_dimension=3, tiled=True
        )
        running = running + local_coeffs
    orthonormal, upper_factor = finish(fine_block, row_count)
    return (orthonormal, running, upper_factor)


def solution(mesh):
    in_specs = (
        P(None, None, "space", "basis", None),
        P("basis", None, "space", None, None),
        P("space", "basis", None),
        P(),
        P(),
        P(),
        P(),
        P(),
        P(),
        P(),
    )
    out_specs = (P(None, None, "space", "basis", None), P("basis", None), P())
    return jax.shard_map(shards, mesh=mesh, in_specs=in_specs, out_specs=out_specs, check_vma=False)
```

profile of v0, /device:TPU:1, one launch (start us, length us, event | category | flops | bytes accessed | tf_op | source)
XLA Modules:
  0.0 749.9 jit_solution(10074327521690366731)
XLA Ops:
  7.3 1.0 copy.71
  8.3 8.8 %collective-permute-start.1 = (f32[16,3,1,8,128]{4,0,3,1,2:T(8,128)S(1)}, f32[16,3,1,8,128]{4,0,3,1,2:T(8,128)S(1)}, u32[]{:S(2)}, u32[]{:S(2)}) collective-permute-start(f32[16,3,1,8,128]{4,0,3,1,2:T(8,128)S(1)} %copy.71), channel_id=1, source_target_pairs={{4,0},{8,4},{12,8},{16,12},{20,16},{24,20},{28,24},{32,28},{36,32}... | collective-permute-start | bytes 589832 | tf_op jit(solution)/shard_map/ppermute | solution.py:19
  17.1 1.9 collective-permute-start
  19.7 1.3 dynamic-slice.13
  21.0 1.3 dynamic-slice.12
  23.7 0.1 scatter-add.4
  23.9 0.1 copy.94
  24.0 0.1 copy.101
  24.1 0.1 copy.100
  24.2 0.1 copy.99
  24.3 0.1 copy.98
  24.4 0.1 copy.97
  24.5 0.1 copy.96
  24.6 0.1 copy.95
  24.7 0.6 multiply_add_fusion
  25.4 0.1 fusion.22
  25.6 0.9 copy-done.1
  26.6 1.3 collective-permute-start.3
  27.9 4.0 collective-permute-start.2
  31.9 1.4 collective-permute-done.2
  33.2 0.2 add_add_fusion.2
  33.4 0.2 add_add_fusion.1
  33.7 0.2 add_add_fusion
  33.9 11.9 %all_gather.6 = f32[16,3,1,32,128]{4,0,3,1,2:T(8,128)S(1)} all-gather(f32[16,3,1,8,128]{4,0,3,1,2:T(8,128)S(1)} %pad_maximum_fusion), channel_id=1, replica_groups=mesh['space'=128,'basis'=4] {'basis'}, dimensions={3}, use_global_device_ids=true | all-gather | bytes 983040 | tf_op jit(solution)/shard_map/all_gather | solution.py:109
  45.8 1.4 convolution_bitcast_fusion.4
  47.2 256.7 %psum.21 = f32[16,16]{0,1:T(8,128)S(1)} all-reduce(f32[16,16]{0,1:T(8,128)S(1)} %convolution_bitcast_fusion.4), channel_id=1, replica_groups=mesh['space'=128,'basis'=4] {'space'}, use_global_device_ids=true, to_apply=%region_0.1 | all-reduce | flops 256 | bytes 2048 | tf_op jit(solution)/shard_map/psum | solution.py:74
  303.9 1.1 convolution_bitcast_fusion.1
  305.1 1.1 copy.129
  306.3 26.9 %reduce-scatter.9.cloned.1.call-done = f32[8,6144]{1,0:T(8,128)} async-done(((f32[32,6144]{1,0:T(8,128)}), f32[8,6144]{1,0:T(8,128)}) %reduce-scatter.9.cloned.1.call-update) | async-done | bytes 196624
  333.2 1.0 copy.108
  334.2 11.1 %all_gather.7 = f32[16,3,1,32,128]{4,0,3,1,2:T(8,128)S(1)} all-gather(f32[16,3,1,8,128]{4,0,3,1,2:T(8,128)S(1)} %copy_subtract_fusion.1), channel_id=1, replica_groups=mesh['space'=128,'basis'=4] {'basis'}, dimensions={3}, use_global_device_ids=true | all-gather | bytes 983040 | tf_op jit(solution)/shard_map/all_gather | solution.py:109
  345.3 1.4 convolution_bitcast_fusion.3
  346.7 256.0 %psum.22 = f32[16,16]{0,1:T(8,128)S(1)} all-reduce(f32[16,16]{0,1:T(8,128)S(1)} %convolution_bitcast_fusion.3), channel_id=1, replica_groups=mesh['space'=128,'basis'=4] {'space'}, use_global_device_ids=true, to_apply=%region_2.3 | all-reduce | flops 256 | bytes 2048 | tf_op jit(solution)/shard_map/psum | solution.py:74
  602.7 1.1 convolution_bitcast_fusion
  603.9 1.1 copy.128
  605.1 0.7 copy.86
  605.8 24.7 %reduce-scatter.11.cloned.1.call-done = f32[8,6144]{1,0:T(8,128)} async-done(((f32[32,6144]{1,0:T(8,128)}), f32[8,6144]{1,0:T(8,128)}) %reduce-scatter.11.cloned.1.call-update) | async-done | bytes 196624
  630.5 1.0 copy.110
  631.5 0.3 convolution_bitcast_fusion.6
  631.8 105.2 %psum.23 = f32[16,16]{0,1:T(8,128)S(1)} all-reduce(f32[16,16]{0,1:T(8,128)S(1)} %convolution_bitcast_fusion.6), channel_id=1, replica_groups=mesh['space'=128,'basis'=4] {'space','basis'}, use_global_device_ids=true, to_apply=%region_4.5 | all-reduce | flops 256 | bytes 2048 | tf_op jit(solution)/shard_map/psum | solution.py:89
  737.1 1.5 cholesky.17
  738.6 0.6 compare_reduce_fusion
  739.2 0.6 fusion.15
  739.9 0.7 copy.87
  740.6 1.2 custom-call.7
  741.8 0.2 convolution_bitcast_fusion.5
  742.0 0.3 convolution_bitcast_fusion.2
  742.3 0.7 copy.85
  (43 shorter events, 0.7 us)
Async XLA Ops:
  7.2 38.7 %copy-start = (f32[16,3,1,32,128]{4,3,2,1,0:T(8,128)S(1)}, f32[16,3,1,32,128]{4,3,2,1,0:T(8,128)}, u32[]{:S(2)}) copy-start(f32[16,3,1,32,128]{4,3,2,1,0:T(8,128)} %param.13) | copy-start | bytes 2359300
  7.2 326.0 %reduce-scatter.9.cloned.1.call-start = ((), (), s32[]{:S(2)}) async-start(), calls=%async_computation.2 | async-start | bytes 983040
  7.2 16.3 %copy-start.4 = (s32[1,8,128]{2,1,0:T(8,128)S(1)}, s32[1,8,128]{2,1,0:T(8,128)}, u32[]{:S(2)}) copy-start(s32[1,8,128]{2,1,0:T(8,128)} %param.14) | copy-start | bytes 12292
  7.2 16.3 %copy-start.5 = (f32[8,3]{0,1:T(4,128)S(1)}, f32[8,3]{0,1:T(4,128)}, u32[]{:S(2)}) copy-start(f32[8,3]{0,1:T(4,128)} %param.16) | copy-start | bytes 292
  7.2 16.3 %copy-start.6 = (f32[8,3]{0,1:T(4,128)S(1)}, f32[8,3]{0,1:T(4,128)}, u32[]{:S(2)}) copy-start(f32[8,3]{0,1:T(4,128)} %param.18) | copy-start | bytes 292
  8.3 18.2 %collective-permute-start.1 = (f32[16,3,1,8,128]{4,0,3,1,2:T(8,128)S(1)}, f32[16,3,1,8,128]{4,0,3,1,2:T(8,128)S(1)}, u32[]{:S(2)}, u32[]{:S(2)}) collective-permute-start(f32[16,3,1,8,128]{4,0,3,1,2:T(8,128)S(1)} %copy.71), channel_id=1, source_target_pairs={{4,0},{8,4},{12,8},{16,12},{20,16},{24,20},{28,24},{32,28},{36,32}... | collective-permute-start | bytes 589832 | tf_op jit(solution)/shard_map/ppermute | solution.py:19
  17.1 8.5 %collective-permute-start = (f32[16,3,1,8,128]{4,0,3,1,2:T(8,128)S(1)}, f32[16,3,1,8,128]{4,0,3,1,2:T(8,128)S(1)}, u32[]{:S(2)}, u32[]{:S(2)}) collective-permute-start(f32[16,3,1,8,128]{4,0,3,1,2:T(8,128)S(1)} %copy.71), channel_id=1, source_target_pairs={{0,4},{4,8},{8,12},{12,16},{16,20},{20,24},{24,28},{28,32},{32,36}... | collective-permute-start | bytes 589832 | tf_op jit(solution)/shard_map/ppermute | solution.py:17
  19.0 4.6 copy-start.3
  19.0 4.6 copy-start.2
  25.5 0.9 copy-start.1
  26.6 5.3 collective-permute-start.3
  27.9 5.4 collective-permute-start.2
  306.3 324.3 %reduce-scatter.11.cloned.1.call-start = ((), (), s32[]{:S(2)}) async-start(), calls=%async_computation.3 | async-start | bytes 983040
Sparse Core Ops, SparseCore 0:
  306.4 26.7 reduce-scatter.8
  605.2 25.2 reduce-scatter.10
where the time goes:
time: 750 us
  blocking collectives  641 us (85%)
  waiting for transfers between devices  53 us (7%)
  between operations  16.4 us (2%)
  starting transfers between devices  16.1 us (2%)
  local copies, waits for them, and re-layouts  12.2 us (2%)
    psum x2, blocking collectives, group_sum(): return lax.psum(partial_value, 'space')  513 us
    psum x1, blocking collectives, finish(): gram_matrix = lax.psum(gram_partial, ('space', 'basis')) / row_count  105 us
    unnamed x4, waiting for transfers between devices  51.6 us
    all_gather x2, blocking collectives, shards(): lax.all_gather(fine_block, 'basis', axis=3, tiled=True)  23 us
  transfers between devices with their start and end apart: 6, of which 3 were waited for; matrix products, arithmetic and copies ran while one was open for 1% of the time, Pallas kernels for 0%

commit v1 on v0

--- a/solution.py
+++ b/solution.py
@@ -106,7 +106,10 @@
         partial_value = jnp.einsum(
             "kcxyz,ncxyz->kn",
             basis,
-            lax.all_gather(fine_block, "basis", axis=3, tiled=True),
+            jnp.concatenate(
+                lax.all_to_all(jnp.stack([fine_block] * lax.axis_size("basis")), "basis", 0, 0),
+                axis=3,
+            ),
             precision=exact_precision,
         )
         local_coeffs = group_sum(partial_value) / row_count

time: 750 us -> 751 us (level)
    all_to_all x0 -> x2, blocking collectives: none -> 26.1 us  [shards(): lax.all_to_all(jnp.stack([fine_block] * lax.axis_size('basis')), 'basis',...]
    all_gather x2 -> x0, blocking collectives: 23 us -> none  [shards(): lax.all_gather(fine_block, 'basis', axis=3, tiled=True)]
where the time goes in v1:
time: 751 us
  blocking collectives  641 us (85%)
  waiting for transfers between devices  53.3 us (7%)
  between operations  16.4 us (2%)
  starting transfers between devices  16.1 us (2%)
  local copies, waits for them, and re-layouts  12.4 us (2%)
    psum x2, blocking collectives, group_sum(): return lax.psum(partial_value, 'space')  510 us
    psum x1, blocking collectives, finish(): gram_matrix = lax.psum(gram_partial, ('space', 'basis')) / row_count  105 us
    unnamed x4, waiting for transfers between devices  51.9 us
    all_to_all x2, blocking collectives, shards(): lax.all_to_all(jnp.stack([fine_block] * lax.axis_size('basis')), 'basis',...  26.1 us
  transfers between devices with their start and end apart: 6, of which 3 were waited for; matrix products, arithmetic and copies ran while one was open for 1% of the time, Pallas kernels for 0%

profile of v1, /device:TPU:1, one launch (start us, length us, event | category | flops | bytes accessed | tf_op | source)
XLA Modules:
  0.0 750.6 jit_solution(15584955501468395583)
XLA Ops:
  7.3 1.0 copy.71
  8.3 8.8 %collective-permute-start.1 = (f32[16,3,1,8,128]{4,0,3,1,2:T(8,128)S(1)}, f32[16,3,1,8,128]{4,0,3,1,2:T(8,128)S(1)}, u32[]{:S(2)}, u32[]{:S(2)}) collective-permute-start(f32[16,3,1,8,128]{4,0,3,1,2:T(8,128)S(1)} %copy.71), channel_id=1, source_target_pairs={{4,0},{8,4},{12,8},{16,12},{20,16},{24,20},{28,24},{32,28},{36,32}... | collective-permute-start | bytes 589832 | tf_op jit(solution)/shard_map/ppermute | solution.py:19
  17.1 1.9 collective-permute-start
  19.7 1.3 dynamic-slice.13
  21.0 1.3 dynamic-slice.12
  23.7 0.1 scatter-add.4
  23.9 0.1 copy.96
  24.0 0.1 copy.103
  24.1 0.1 copy.102
  24.2 0.1 copy.101
  24.3 0.1 copy.100
  24.4 0.1 copy.99
  24.5 0.1 copy.98
  24.6 0.1 copy.97
  24.7 0.6 multiply_add_fusion
  25.4 0.1 fusion.22
  25.6 0.9 copy-done.1
  26.6 1.3 collective-permute-start.3
  27.9 4.0 collective-permute-start.2
  31.9 1.4 collective-permute-done.2
  33.2 0.2 add_add_fusion.2
  33.4 0.2 add_add_fusion.1
  33.7 0.2 add_add_fusion
  34.0 13.3 %all_to_all.10 = f32[4,16,3,1,8,128]{5,1,4,2,3,0:T(8,128)S(1)} all-to-all(f32[4,16,3,1,8,128]{5,1,4,2,3,0:T(8,128)S(1)} %stack.10), channel_id=1, replica_groups=mesh['space'=128,'basis'=4] {'basis'}, dimensions={0} | all-to-all | bytes 1572864 | tf_op jit(solution)/shard_map/all_to_all | solution.py:110
  47.3 1.4 convolution_bitcast_fusion.4
  48.7 255.5 %psum.21 = f32[16,16]{0,1:T(8,128)S(1)} all-reduce(f32[16,16]{0,1:T(8,128)S(1)} %convolution_bitcast_fusion.4), channel_id=1, replica_groups=mesh['space'=128,'basis'=4] {'space'}, use_global_device_ids=true, to_apply=%region_0.1 | all-reduce | flops 256 | bytes 2048 | tf_op jit(solution)/shard_map/psum | solution.py:74
  304.3 1.1 convolution_bitcast_fusion.1
  305.5 1.1 copy.139
  306.7 27.4 %reduce-scatter.9.cloned.1.call-done = f32[8,6144]{1,0:T(8,128)} async-done(((f32[32,6144]{1,0:T(8,128)}), f32[8,6144]{1,0:T(8,128)}) %reduce-scatter.9.cloned.1.call-update) | async-done | bytes 196624
  334.1 1.0 copy.110
  335.2 12.8 %all_to_all.11 = f32[4,16,3,1,8,128]{5,1,4,2,3,0:T(8,128)S(1)} all-to-all(f32[4,16,3,1,8,128]{5,1,4,2,3,0:T(8,128)S(1)} %stack.11), channel_id=1, replica_groups=mesh['space'=128,'basis'=4] {'basis'}, dimensions={0} | all-to-all | bytes 1572864 | tf_op jit(solution)/shard_map/all_to_all | solution.py:110
  348.1 1.4 convolution_bitcast_fusion.3
  349.5 254.3 %psum.22 = f32[16,16]{0,1:T(8,128)S(1)} all-reduce(f32[16,16]{0,1:T(8,128)S(1)} %convolution_bitcast_fusion.3), channel_id=1, replica_groups=mesh['space'=128,'basis'=4] {'space'}, use_global_device_ids=true, to_apply=%region_2.3 | all-reduce | flops 256 | bytes 2048 | tf_op jit(solution)/shard_map/psum | solution.py:74
  603.8 1.1 convolution_bitcast_fusion
  605.0 1.1 copy.138
  606.2 0.7 copy.88
  606.8 24.4 %reduce-scatter.11.cloned.1.call-done = f32[8,6144]{1,0:T(8,128)} async-done(((f32[32,6144]{1,0:T(8,128)}), f32[8,6144]{1,0:T(8,128)}) %reduce-scatter.11.cloned.1.call-update) | async-done | bytes 196624
  631.3 1.0 copy.112
  632.2 0.4 convolution_bitcast_fusion.6
  632.6 105.2 %psum.23 = f32[16,16]{0,1:T(8,128)S(1)} all-reduce(f32[16,16]{0,1:T(8,128)S(1)} %convolution_bitcast_fusion.6), channel_id=1, replica_groups=mesh['space'=128,'basis'=4] {'space','basis'}, use_global_device_ids=true, to_apply=%region_4.5 | all-reduce | flops 256 | bytes 2048 | tf_op jit(solution)/shard_map/psum | solution.py:89
  737.8 1.5 cholesky.17
  739.3 0.6 compare_reduce_fusion
  740.0 0.6 fusion.14
  740.6 0.7 copy.89
  741.3 1.2 custom-call.7
  742.5 0.2 convolution_bitcast_fusion.5
  742.7 0.3 convolution_bitcast_fusion.2
  743.0 0.7 copy.87
  (47 shorter events, 0.9 us)
Async XLA Ops:
  7.2 40.2 %copy-start = (f32[16,3,1,32,128]{4,3,2,1,0:T(8,128)S(1)}, f32[16,3,1,32,128]{4,3,2,1,0:T(8,128)}, u32[]{:S(2)}) copy-start(f32[16,3,1,32,128]{4,3,2,1,0:T(8,128)} %param.13) | copy-start | bytes 2359300
  7.2 326.9 %reduce-scatter.9.cloned.1.call-start = ((), (), s32[]{:S(2)}) async-start(), calls=%async_computation.4 | async-start | bytes 983040
  7.2 16.3 %copy-start.4 = (s32[1,8,128]{2,1,0:T(8,128)S(1)}, s32[1,8,128]{2,1,0:T(8,128)}, u32[]{:S(2)}) copy-start(s32[1,8,128]{2,1,0:T(8,128)} %param.14) | copy-start | bytes 12292
  7.2 16.3 %copy-start.5 = (f32[8,3]{0,1:T(4,128)S(1)}, f32[8,3]{0,1:T(4,128)}, u32[]{:S(2)}) copy-start(f32[8,3]{0,1:T(4,128)} %param.16) | copy-start | bytes 292
  7.2 16.3 %copy-start.6 = (f32[8,3]{0,1:T(4,128)S(1)}, f32[8,3]{0,1:T(4,128)}, u32[]{:S(2)}) copy-start(f32[8,3]{0,1:T(4,128)} %param.18) | copy-start | bytes 292
  8.3 18.2 %collective-permute-start.1 = (f32[16,3,1,8,128]{4,0,3,1,2:T(8,128)S(1)}, f32[16,3,1,8,128]{4,0,3,1,2:T(8,128)S(1)}, u32[]{:S(2)}, u32[]{:S(2)}) collective-permute-start(f32[16,3,1,8,128]{4,0,3,1,2:T(8,128)S(1)} %copy.71), channel_id=1, source_target_pairs={{4,0},{8,4},{12,8},{16,12},{20,16},{24,20},{28,24},{32,28},{36,32}... | collective-permute-start | bytes 589832 | tf_op jit(solution)/shard_map/ppermute | solution.py:19
  17.1 8.5 %collective-permute-start = (f32[16,3,1,8,128]{4,0,3,1,2:T(8,128)S(1)}, f32[16,3,1,8,128]{4,0,3,1,2:T(8,128)S(1)}, u32[]{:S(2)}, u32[]{:S(2)}) collective-permute-start(f32[16,3,1,8,128]{4,0,3,1,2:T(8,128)S(1)} %copy.71), channel_id=1, source_target_pairs={{0,4},{4,8},{8,12},{12,16},{16,20},{20,24},{24,28},{28,32},{32,36}... | collective-permute-start | bytes 589832 | tf_op jit(solution)/shard_map/ppermute | solution.py:17
  19.0 4.6 copy-start.3
  19.0 4.6 copy-start.2
  25.5 0.9 copy-start.1
  26.6 5.3 collective-permute-start.3
  27.9 5.4 collective-permute-start.2
  306.6 324.6 %reduce-scatter.11.cloned.1.call-start = ((), (), s32[]{:S(2)}) async-start(), calls=%async_computation.5 | async-start | bytes 983040
Sparse Core Ops, SparseCore 0:
  306.8 27.3 reduce-scatter.8
  606.3 24.9 reduce-scatter.10
